TPU v7x, 256 devices: a whole 4x4x8 slice. The times are simulated.
256 devices in a mesh: grid: 32 (over z, y_lo, core), band: 8 (over y_hi, x).
Axes of the slice: x: 4, y: 4 (y_hi: 2, y_lo: 2; y = y_hi * 2 + y_lo), z: 8, core: 2. Of those that a mesh axis runs over, the one named last changes fastest.
Arguments:
- orbitals: float32 [32, 96, 9216], P('band', 'grid'), may hold values from -6 to 6
- sign_vectors: int32 [64, 96, 9216], P('band', 'grid'), may hold values from -1 to 1, as said below
- potential: float32 [96, 9216], P('grid'), may hold values from -0.45 to 0.45
- cheb_coefs: float32 [7], replicated, may hold values from 0.2 to 1
Outputs:
- density: float32 [96, 9216], P('grid', 'band')
- margins: float32 [32, 64], P(None, 'band')
- noise_out: float32 [64, 96, 9216], P('band', 'grid')
Inputs may be any that keep to these rules, and one draw needn't show every extreme that they name: `sign_vectors`: every entry is -1 or 1.
All inputs are finite; a program needn't handle non-finite values.
Results may differ from a plain program's by a relative error of at most 0.00012.
Values sent between devices are 32-bit elements; how exact they have to be, the bound alone decides.
A program may use at most 64 MiB of HBM per device.

v0:
```python
import math

import jax
import jax.numpy as jnp
from jax import lax
from jax.sharding import PartitionSpec as P

NG = 96
ORDER = 6


def kinetic_matrix():
    indices = jnp.arange(NG, dtype=jnp.int32)
    product_mod = indices[:, None] * indices[None, :] % NG
    phases = 2.0 * math.pi / NG * product_mod.astype(jnp.float32)
    hartley = (jnp.cos(phases) + jnp.sin(phases)) / math.sqrt(NG)
    wavenumber = jnp.minimum(indices, NG - indices).astype(jnp.float32) / (NG / 2.0)
    spectrum = (wavenumber * wavenumber - 0.5) / 3.0
    return jnp.dot(hartley, spectrum[:, None] * hartley, precision=lax.Precision.HIGHEST)


def apply_operator(current, field_slab, kinetic):
    high = lax.Precision.HIGHEST
    along_z = jnp.einsum("vpyz,wz->vpyw", current, kinetic, precision=high)
    along_y = jnp.einsum("vpyz,wy->vpwz", current, kinetic, precision=high)
    turned = jnp.einsum(
        "vxqz,wx->vwqz",
        lax.all_to_all(current, "grid", split_axis=2, concat_axis=1, tiled=True),
        kinetic,
        precision=high,
    )
    along_x = lax.all_to_all(turned, "grid", split_axis=1, concat_axis=2, tiled=True)
    return along_x + along_y + along_z + field_slab[None] * current


def chebyshev(vectors, field_slab, kinetic, cheb_coefs):
    previous = vectors
    current = apply_operator(vectors, field_slab, kinetic)
    filtered = cheb_coefs[0] * previous + cheb_coefs[1] * current
    for order_index in range(2, ORDER + 1):
        following = 2.0 * apply_operator(current, field_slab, kinetic) - previous
        filtered = filtered + cheb_coefs[order_index] * following
        previous, current = (current, following)
    return filtered


def local(orbitals, sign_vectors, potential, cheb_coefs):
    high = lax.Precision.HIGHEST
    planes = orbitals.shape[1]
    orbital_count = orbitals.shape[0]
    noise_count = sign_vectors.shape[0]
    band_count = lax.axis_size("band")
    total_vectors = float((orbital_count + noise_count) * band_count)
    scale_root = math.sqrt(float(NG) ** 3)
    kinetic = kinetic_matrix()
    noise = sign_vectors.astype(jnp.float32)
    gathered = lax.all_gather(orbitals, "band", axis=0, tiled=True)
    partial_margin = jnp.einsum("ipn,spn->is", gathered, noise, precision=high)
    margins = lax.psum(partial_margin, "grid") / scale_root
    correction = jnp.einsum("is,ipn->spn", margins, gathered, precision=high)
    projected = noise - correction / scale_root
    field_slab = potential.reshape(planes, NG, NG)
    joined = jnp.concatenate([orbitals, projected], 0).reshape(
        orbital_count + noise_count, planes, NG, NG
    )
    results = chebyshev(joined, field_slab, kinetic, cheb_coefs)
    orbital_out = results[:orbital_count]
    noise_result = results[orbital_count:]
    squares = (
        jnp.sum(orbital_out * orbital_out, axis=0) + jnp.sum(noise_result * noise_result, axis=0)
    ) / total_vectors
    squares = squares.reshape(planes, NG * NG)
    summed = lax.psum(squares, "band")
    share_width = squares.shape[1] // band_count
    density = lax.dynamic_slice_in_dim(summed, lax.axis_index("band") * share_width, share_width, 1)
    return (density, margins, noise_result.reshape(noise_count, planes, NG * NG))


def solution(mesh):
    return jax.shard_map(
        local,
        mesh=mesh,
        in_specs=(P("band", "grid", None), P("band", "grid", None), P("grid", None), P()),
        out_specs=(P("grid", "band"), P(None, "band"), P("band", "grid", None)),
        check_vma=False,
    )
```

profile of v0, /device:TPU:2, one launch (start us, length us, event | category | flops | bytes accessed | tf_op | source)
XLA Modules:
  0.0 1151.4 jit_solution(5754088638190613420)
XLA Ops:
  9.4 84.6 %all-gather.2.cloned.1.call-done = f32[32,3,9216]{2,1,0:T(4,128)} async-done(((f32[4,3,9216]{2,1,0:T(4,128)}), f32[32,3,9216]{2,1,0:T(4,128)}) %all-gather.2.cloned.1.call-update) | async-done | bytes 3538960 | tf_op jit(solution)/shard_map/all_gather | solution.py:57
  94.0 5.7 fusion.31
  99.7 55.4 %psum.14 = f32[32,8]{0,1:T(8,128)S(1)} all-reduce(f32[32,8]{0,1:T(8,128)S(1)} %fusion.31), channel_id=1, replica_groups=mesh['grid'=32,'band'=8] {'grid'}, use_global_device_ids=true, to_apply=%region_0.1 | all-reduce | flops 256 | bytes 2048 | tf_op jit(solution)/shard_map/psum | solution.py:59
  155.1 5.2 fusion
  163.8 5.2 all-to-all-start
  169.4 55.3 %all-to-all-done = f32[12,3,96,96]{3,1,0,2:T(4,128)} async-done(((f32[12,3,96,96]{3,1,0,2:T(4,128)}), f32[12,3,96,96]{3,1,0,2:T(4,128)}, u32[]{:S(2)}, u32[]{:S(2)}) %all-to-all-start) | async-done | bytes 1327136 | tf_op jit(solution)/shard_map/all_to_all | solution.py:28
  238.3 5.2 all-to-all-start.1
  247.1 52.1 %all-to-all-done.1 = f32[12,96,3,96]{3,2,0,1:T(4,128)} async-done(((f32[12,96,3,96]{3,2,0,1:T(4,128)}), f32[12,96,3,96]{3,2,0,1:T(4,128)}, u32[]{:S(2)}, u32[]{:S(2)}) %all-to-all-start.1) | async-done | bytes 1327136 | tf_op jit(solution)/shard_map/all_to_all | solution.py:32
  312.3 61.8 %all_to_all.216 = f32[12,3,96,96]{3,1,0,2:T(4,128)S(1)} all-to-all(f32[12,3,96,96]{3,1,0,2:T(4,128)S(1)} %copy.57), channel_id=1, replica_groups=mesh['grid'=32,'band'=8] {'grid'}, dimensions={2} | all-to-all | bytes 2654208 | tf_op jit(solution)/shard_map/all_to_all | solution.py:28
  385.9 5.0 all-to-all-start.3
  394.5 53.7 %all-to-all-done.3 = f32[12,96,3,96]{3,2,0,1:T(4,128)} async-done(((f32[12,96,3,96]{3,2,0,1:T(4,128)}), f32[12,96,3,96]{3,2,0,1:T(4,128)}, u32[]{:S(2)}, u32[]{:S(2)}) %all-to-all-start.3) | async-done | bytes 1327136 | tf_op jit(solution)/shard_map/all_to_all | solution.py:32
  461.4 60.2 %all_to_all.217 = f32[12,3,96,96]{3,1,0,2:T(4,128)S(1)} all-to-all(f32[12,3,96,96]{3,1,0,2:T(4,128)S(1)} %copy.64), channel_id=1, replica_groups=mesh['grid'=32,'band'=8] {'grid'}, dimensions={2} | all-to-all | bytes 2654208 | tf_op jit(solution)/shard_map/all_to_all | solution.py:28
  533.5 5.2 all-to-all-start.5
  538.7 4.3 fusion.66
  543.0 53.0 %all-to-all-done.5 = f32[12,96,3,96]{3,2,0,1:T(4,128)} async-done(((f32[12,96,3,96]{3,2,0,1:T(4,128)}), f32[12,96,3,96]{3,2,0,1:T(4,128)}, u32[]{:S(2)}, u32[]{:S(2)}) %all-to-all-start.5) | async-done | bytes 1327136 | tf_op jit(solution)/shard_map/all_to_all | solution.py:32
  603.9 5.1 fusion.21
  610.2 60.2 %all_to_all.218 = f32[12,3,96,96]{3,1,0,2:T(4,128)S(1)} all-to-all(f32[12,3,96,96]{3,1,0,2:T(4,128)S(1)} %copy.70), channel_id=1, replica_groups=mesh['grid'=32,'band'=8] {'grid'}, dimensions={2} | all-to-all | bytes 2654208 | tf_op jit(solution)/shard_map/all_to_all | solution.py:28
  682.3 5.0 all-to-all-start.7
  687.3 4.3 fusion.67
  691.5 53.0 %all-to-all-done.7 = f32[12,96,3,96]{3,2,0,1:T(4,128)} async-done(((f32[12,96,3,96]{3,2,0,1:T(4,128)}), f32[12,96,3,96]{3,2,0,1:T(4,128)}, u32[]{:S(2)}, u32[]{:S(2)}) %all-to-all-start.7) | async-done | bytes 1327136 | tf_op jit(solution)/shard_map/all_to_all | solution.py:32
  752.4 5.6 fusion.17
  759.3 60.2 %all_to_all.219 = f32[12,3,96,96]{3,1,0,2:T(4,128)S(1)} all-to-all(f32[12,3,96,96]{3,1,0,2:T(4,128)S(1)} %copy.76), channel_id=1, replica_groups=mesh['grid'=32,'band'=8] {'grid'}, dimensions={2} | all-to-all | bytes 2654208 | tf_op jit(solution)/shard_map/all_to_all | solution.py:28
  831.3 5.0 all-to-all-start.9
  836.3 4.2 fusion.68
  840.6 53.1 %all-to-all-done.9 = f32[12,96,3,96]{3,2,0,1:T(4,128)} async-done(((f32[12,96,3,96]{3,2,0,1:T(4,128)}), f32[12,96,3,96]{3,2,0,1:T(4,128)}, u32[]{:S(2)}, u32[]{:S(2)}) %all-to-all-start.9) | async-done | bytes 1327136 | tf_op jit(solution)/shard_map/all_to_all | solution.py:32
  901.5 5.6 fusion.13
  908.3 60.2 %all_to_all.220 = f32[12,3,96,96]{3,1,0,2:T(4,128)S(1)} all-to-all(f32[12,3,96,96]{3,1,0,2:T(4,128)S(1)} %copy.82), channel_id=1, replica_groups=mesh['grid'=32,'band'=8] {'grid'}, dimensions={2} | all-to-all | bytes 2654208 | tf_op jit(solution)/shard_map/all_to_all | solution.py:28
  980.4 4.9 all-to-all-start.11
  986.3 4.3 fusion.69
  990.7 52.0 %all-to-all-done.11 = f32[12,96,3,96]{3,2,0,1:T(4,128)} async-done(((f32[12,96,3,96]{3,2,0,1:T(4,128)}), f32[12,96,3,96]{3,2,0,1:T(4,128)}, u32[]{:S(2)}, u32[]{:S(2)}) %all-to-all-start.11) | async-done | bytes 1327136 | tf_op jit(solution)/shard_map/all_to_all | solution.py:32
  1050.5 11.8 %fusion.9 = f32[12,3,96,96]{3,2,1,0:T(8,128)S(1)} fusion(f32[12,3,96,96]{3,2,1,0:T(8,128)} %copy-done.2, f32[12,3,96,96]{3,2,1,0:T(8,128)} %fusion.69, f32[12,3,96,96]{3,2,1,0:T(8,128)} %all_to_all.203, f32[12,3,96,96]{3,2,1,0:T(8,128)} %copy-done.3, f32[12,3,96,96]{3,2,1,0:T(8,128)} %copy-done.1, f32[12,3,96,96]{3,2,1,0:T(8,128)} %copy-done, ...), kind=kOutput, calls=%fused_computation.12 | convolution fusion | flops 388509696 | bytes 12091420 | tf_op jit(solution)/shard_map/vpyz,wy->vpwz/dot_general | solution.py:25
  1065.9 76.9 %all-reduce.2.cloned.1.call-done = f32[3,9216]{1,0:T(4,128)} async-done(((f32[3,9216]{1,0:T(4,128)}), f32[3,9216]{1,0:T(4,128)}) %all-reduce.2.cloned.1.call-update) | async-done | bytes 110608 | tf_op jit(solution)/shard_map/psum | solution.py:73
  (85 shorter events, 153.4 us)
Async XLA Ops:
  7.2 86.8 %copy-start.5 = (s32[8,3,9216]{2,0,1:T(8,128)S(1)}, s32[8,3,9216]{2,0,1:T(8,128)}, u32[]{:S(2)}) copy-start(s32[8,3,9216]{2,0,1:T(8,128)} %param.5) | copy-start | bytes 2654212
  7.2 86.8 %all-gather.2.cloned.1.call-start = ((), (), s32[]{:S(2)}) async-start(), calls=%async_computation.12 | async-start | bytes 5308416 | tf_op jit(solution)/shard_map/all_gather | solution.py:57
  155.1 5.2 copy-start.9
  155.1 5.2 copy-start.6
  163.8 60.9 %all-to-all-start = ((f32[12,3,96,96]{3,1,0,2:T(4,128)}), f32[12,3,96,96]{3,1,0,2:T(4,128)}, u32[]{:S(2)}, u32[]{:S(2)}) async-start(f32[12,3,96,96]{3,1,0,2:T(4,128)} %copy.48), calls=%async_computation | async-start | bytes 4718592 | tf_op jit(solution)/shard_map/all_to_all | solution.py:28
  169.4 74.9 %copy-start.4 = (f32[96,96,1,1]{1,0,3,2:T(8,128)}, f32[96,96,1,1]{1,0,3,2:T(8,128)S(1)}, u32[]{:S(2)}) copy-start(f32[96,96,1,1]{1,0,3,2:T(8,128)S(1)} %convolution_bitcast_fusion.6) | copy-start | bytes 110596
  238.3 5.2 copy-start.7
  238.3 60.9 %all-to-all-start.1 = ((f32[12,96,3,96]{3,2,0,1:T(4,128)}), f32[12,96,3,96]{3,2,0,1:T(4,128)}, u32[]{:S(2)}, u32[]{:S(2)}) async-start(f32[12,96,3,96]{3,2,0,1:T(4,128)} %copy.51), calls=%async_computation.1 | async-start | bytes 4718592 | tf_op jit(solution)/shard_map/all_to_all | solution.py:32
  385.9 62.3 %all-to-all-start.3 = ((f32[12,96,3,96]{3,2,0,1:T(4,128)}), f32[12,96,3,96]{3,2,0,1:T(4,128)}, u32[]{:S(2)}, u32[]{:S(2)}) async-start(f32[12,96,3,96]{3,2,0,1:T(4,128)} %copy.60), calls=%async_computation.3 | async-start | bytes 4718592 | tf_op jit(solution)/shard_map/all_to_all | solution.py:32
  460.2 1.3 copy-start
  533.5 62.5 %all-to-all-start.5 = ((f32[12,96,3,96]{3,2,0,1:T(4,128)}), f32[12,96,3,96]{3,2,0,1:T(4,128)}, u32[]{:S(2)}, u32[]{:S(2)}) async-start(f32[12,96,3,96]{3,2,0,1:T(4,128)} %copy.67), calls=%async_computation.5 | async-start | bytes 4718592 | tf_op jit(solution)/shard_map/all_to_all | solution.py:32
  609.0 1.2 copy-start.1
  682.3 62.3 %all-to-all-start.7 = ((f32[12,96,3,96]{3,2,0,1:T(4,128)}), f32[12,96,3,96]{3,2,0,1:T(4,128)}, u32[]{:S(2)}, u32[]{:S(2)}) async-start(f32[12,96,3,96]{3,2,0,1:T(4,128)} %copy.73), calls=%async_computation.7 | async-start | bytes 4718592 | tf_op jit(solution)/shard_map/all_to_all | solution.py:32
  758.0 1.3 copy-start.2
  831.3 62.3 %all-to-all-start.9 = ((f32[12,96,3,96]{3,2,0,1:T(4,128)}), f32[12,96,3,96]{3,2,0,1:T(4,128)}, u32[]{:S(2)}, u32[]{:S(2)}) async-start(f32[12,96,3,96]{3,2,0,1:T(4,128)} %copy.79), calls=%async_computation.9 | async-start | bytes 4718592 | tf_op jit(solution)/shard_map/all_to_all | solution.py:32
  907.1 1.2 copy-start.3
  980.4 5.2 copy-start.8
  980.4 62.2 %all-to-all-start.11 = ((f32[12,96,3,96]{3,2,0,1:T(4,128)}), f32[12,96,3,96]{3,2,0,1:T(4,128)}, u32[]{:S(2)}, u32[]{:S(2)}) async-start(f32[12,96,3,96]{3,2,0,1:T(4,128)} %copy.85), calls=%async_computation.11 | async-start | bytes 4718592 | tf_op jit(solution)/shard_map/all_to_all | solution.py:32
  985.4 157.4 %all-reduce.2.cloned.1.call-start = ((), (), s32[]{:S(2)}) async-start(), calls=%async_computation.13 | async-start | bytes 294912 | tf_op jit(solution)/shard_map/psum | solution.py:73
Sparse Core Ops, SparseCore 0:
  11.2 82.7 all-gather.1
  1063.6 79.1 all-reduce.1
where the time goes:
time: 1160 us; the launch traced here: 1150 us
  waiting for transfers between devices  534 us (46%)
  blocking collectives  358 us (31%)
  local copies, waits for them, and re-layouts  119 us (10%)
  matrix products  89.5 us (8%)
  starting transfers between devices  35.8 us (3%)
  between operations  14.9 us (1%)
    all_to_all x6, waiting for transfers between devices, apply_operator(): lax.all_to_all(turned, 'grid', split_axis=1, concat_axis=2, tiled=True)  317 us
    all_to_all x5, blocking collectives, apply_operator(): lax.all_to_all(current, 'grid', split_axis=2, concat_axis=1, tiled=True)  303 us
    all_gather x1, waiting for transfers between devices, local(): gathered = lax.all_gather(orbitals, 'band', axis=0, tiled=True)  84.6 us
    psum x1, waiting for transfers between devices, local(): summed = lax.psum(squares, 'band')  76.9 us
    psum x1, blocking collectives, local(): margins = lax.psum(partial_margin, 'grid') / scale_root  55.4 us
    all_to_all x1, waiting for transfers between devices, apply_operator(): lax.all_to_all(current, 'grid', split_axis=2, concat_axis=1, tiled=True)  55.3 us
    all_to_all x12, local copies, waits for them, and re-layouts, apply_operator(): lax.all_to_all(turned, 'grid', split_axis=1, concat_axis=2, tiled=True)  47 us
    all_to_all x12, local copies, waits for them, and re-layouts, apply_operator(): lax.all_to_all(current, 'grid', split_axis=2, concat_axis=1, tiled=True)  38.6 us
  transfers between devices with their start and end apart: 9, of which 9 were waited for; matrix products, arithmetic and copies ran while one was open for 2% of the time, Pallas kernels for 0%

commit v1 on v0

v1 whole, which is shorter than its diff:
```python
import math

import jax
import jax.numpy as jnp
import ml_dtypes
import numpy as np
from jax import lax
from jax.experimental import pallas as pl
from jax.experimental.pallas import tpu as pltpu
from jax.sharding import PartitionSpec as P

NG = 96
ORDER = 6
ROWS = 72
XS = 104
UX, UY, UR = 24, 6, 8
MESH = pl.DeviceIdType.MESH
ORB_OWNER = tuple(8 * i + 2 * (1 - i % 2) for i in range(4))
STO_OWNER = tuple(4 * s + 2 * ((s // 2) % 2) for s in range(8))


def tables():
    index = np.arange(NG)
    phase = 2.0 * np.pi / NG * ((index[:, None] * index[None, :]) % NG)
    hartley = (np.cos(phase) + np.sin(phase)) / math.sqrt(NG)
    wave = np.minimum(index, NG - index) / (NG / 2.0)
    doubled = 2.0 * (hartley @ (((wave * wave - 0.5) / 3.0)[:, None] * hartley))
    high = doubled.astype(ml_dtypes.bfloat16)
    low = (doubled - high.astype(np.float64)).astype(ml_dtypes.bfloat16)

    def left(order):
        h, l = high[order][:, order], low[order][:, order]
        return np.block([[h, h], [l, l]])

    right = np.zeros((256, 256), ml_dtypes.bfloat16)
    for at in (0, 128):
        right[at : at + NG, 0:NG] = high
        right[at : at + NG, 128 : 128 + NG] = low
    y_order = np.array([4 * (q % 24) + q // 24 for q in range(NG)])
    return left(index), left(y_order), right


def halves(t):
    high = t.astype(jnp.bfloat16)
    return high, (t - high.astype(jnp.float32)).astype(jnp.bfloat16)


def left_mul(matrix, a, b):
    right = jnp.concatenate(
        [jnp.concatenate([a[0], b[0]], 1), jnp.concatenate([a[1], b[1]], 1)], 0
    )
    out = jnp.dot(matrix, right, preferred_element_type=jnp.float32)
    out = out[:NG] + out[NG:]
    return out[:, :128], out[:, 128:]


def spread(a, lane):
    zero = jnp.zeros((24, 128), jnp.float32)
    one = jnp.where(lane < 32, pltpu.roll(a[0], 32, 1), pltpu.roll(a[1], 32, 1))
    two = jnp.where(lane < 64, pltpu.roll(a[1], 64, 1), pltpu.roll(a[2], 64, 1))
    parts = (a[0], one, two, pltpu.roll(a[2], 96, 1))
    return [jnp.where(lane < 96, part, zero) for part in parts]


def pack(b, lane):
    one = pltpu.roll(b[1], 96, 1)
    two = pltpu.roll(b[2], 64, 1)
    return (
        jnp.where(lane < 96, b[0], one),
        jnp.where(lane < 64, one, two),
        jnp.where(lane < 32, two, pltpu.roll(b[3], 32, 1)),
    )


def quarter(x, j):
    return pl.ds(pl.multiple_of(x * XS + 24 * j, 8), 24)


def filter_vector(land, pot_ref, kx_ref, ky_ref, wz_ref, coef_ref, T, W, FI, PO):
    lane = lax.broadcasted_iota(jnp.int32, (24, 128), 1)
    first_coef = coef_ref[0]

    @pl.loop(0, NG, step=UR)
    def _(base):
        for u in range(UR):
            x = base + u
            for j, part in enumerate(spread([land[x, pl.ds(k, 24, stride=3), :] for k in range(3)], lane)):
                T[0, quarter(x, j), :] = part
                FI[quarter(x, j), :] = first_coef * part
            for j, part in enumerate(spread([pot_ref[x, pl.ds(k, 24, stride=3), :] for k in range(3)], lane)):
                PO[quarter(x, j), :] = 2.0 * part

    @pl.loop(0, ORDER)
    def _(k):
        now = lax.rem(k, 2)
        other = 1 - now
        alpha = jnp.where(k == 0, 0.5, 1.0)
        beta = jnp.where(k == 0, 0.0, 1.0)
        coef = coef_ref[k + 1]

        @pl.loop(0, NG, step=2 * UX)
        def _(base):
            for u in range(UX):
                y = base + 2 * u
                columns = [pl.ds(y + q, NG, stride=XS) for q in range(2)]
                outs = left_mul(kx_ref[...], *[halves(T[now, c, :]) for c in columns])
                for c, out in zip(columns, outs):
                    W[c, :] = out

        @pl.loop(0, NG, step=2 * UY)
        def _(base):
            rows = [pl.ds(pl.multiple_of((base + q) * XS, 8), NG) for q in range(2 * UY)]
            held = [T[now, r, :] for r in rows]
            split = [halves(t) for t in held]
            along_y = []
            for u in range(UY):
                along_y += left_mul(ky_ref[...], split[2 * u], split[2 * u + 1])
            stacked = jnp.concatenate([jnp.concatenate(pair, 1) for pair in split], 0)
            along_z = jnp.dot(stacked, wz_ref[...], preferred_element_type=jnp.float32)
            for q, r in enumerate(rows):
                z = along_z[NG * q : NG * (q + 1)]
                total = z[:, :128] + z[:, 128:] + along_y[q] + W[r, :] + PO[r, :] * held[q]
                following = alpha * total - beta * T[other, r, :]
                T[other, r, :] = following
                FI[r, :] = FI[r, :] + coef * following

    @pl.loop(0, NG, step=UR)
    def _(base):
        for u in range(UR):
            x = base + u
            for k, part in enumerate(pack([FI[quarter(x, j), :] for j in range(4)], lane)):
                land[x, pl.ds(k, 24, stride=3), :] = part


def filter_kernel(
    orb_ref, sto_ref, pot_ref, kx_ref, ky_ref, wz_ref, coef_ref, orb_out, sto_out,
    land, T, W, FI, PO, send_sems, land_sem, orb_sem, sto_sem, out_sem,
):
    me = lax.axis_index("grid")
    level = me // 4
    planes = land.at[pl.ds(3 * me, 3)]
    sources = [(orb_ref.at[:, :, i, :], t) for i, t in enumerate(ORB_OWNER)]
    sources += [(sto_ref.at[:, :, s, :], t) for s, t in enumerate(STO_OWNER)]

    def to_owner(v):
        return pltpu.make_async_remote_copy(
            src_ref=sources[v][0], dst_ref=planes, send_sem=send_sems.at[v], recv_sem=land_sem,
            device_id={"grid": sources[v][1]}, device_id_type=MESH,
        )

    for v in range(12):
        @pl.when(me != sources[v][1])
        def _():
            to_owner(v).start()

        @pl.when(me == sources[v][1])
        def _():
            pltpu.make_async_copy(sources[v][0], planes, land_sem).start()

    turned = (level // 2) % 2
    row = (me // 2) % 2
    first_core = me % 2 == 0
    is_sto = jnp.logical_and(first_core, row == turned)
    is_orb = jnp.logical_and(first_core, jnp.logical_and(row != turned, level % 2 == 0))

    @pl.when(jnp.logical_or(is_sto, is_orb))
    def _():
        pltpu.make_async_copy(land, land, land_sem).wait()
        filter_vector(land, pot_ref, kx_ref, ky_ref, wz_ref, coef_ref, T, W, FI, PO)

    def hand_back(out, at, sem):
        @pl.loop(0, 32)
        def _(d):
            src = land.at[pl.ds(3 * d, 3)]

            @pl.when(d != me)
            def _():
                pltpu.make_async_remote_copy(
                    src_ref=src, dst_ref=out.at[:, :, at, :], send_sem=out_sem, recv_sem=sem,
                    device_id={"grid": d}, device_id_type=MESH,
                ).start()

            @pl.when(d == me)
            def _():
                pltpu.make_async_copy(src, out.at[:, :, at, :], sem).start()

        sent = land.at[pl.ds(0, 93)]
        pltpu.make_async_copy(sent, sent, out_sem).wait()

    for i in range(4):
        @pl.when(me == ORB_OWNER[i])
        def _():
            hand_back(orb_out, i, orb_sem)

    for s in range(8):
        @pl.when(me == STO_OWNER[s])
        def _():
            hand_back(sto_out, s, sto_sem)

    pltpu.make_async_copy(orb_out, orb_out, orb_sem).wait()
    pltpu.make_async_copy(sto_out, sto_out, sto_sem).wait()
    for v in range(12):
        @pl.when(me != sources[v][1])
        def _():
            to_owner(v).wait_send()


def filter_all(orbitals, noise, potential, coefs):
    vmem = pl.BlockSpec(memory_space=pltpu.VMEM)
    anywhere = pl.BlockSpec(memory_space=pl.ANY)
    f32 = jnp.float32
    field = pltpu.VMEM((NG * XS, 128), f32)
    return pl.pallas_call(
        filter_kernel,
        out_shape=(
            jax.ShapeDtypeStruct((3, ROWS, 4, 128), f32),
            jax.ShapeDtypeStruct((3, ROWS, 8, 128), f32),
        ),
        in_specs=[anywhere, anywhere] + [vmem] * 4 + [pl.BlockSpec(memory_space=pltpu.SMEM)],
        out_specs=(anywhere, anywhere),
        scratch_shapes=[
            pltpu.VMEM((NG, ROWS, 128), f32),
            pltpu.VMEM((2, NG * XS, 128), f32),
            field, field, field,
            pltpu.SemaphoreType.DMA((12,)),
            pltpu.SemaphoreType.DMA, pltpu.SemaphoreType.DMA,
            pltpu.SemaphoreType.DMA, pltpu.SemaphoreType.DMA,
        ],
        compiler_params=pltpu.CompilerParams(
            vmem_limit_bytes=56 * 2**20, has_side_effects=True
        ),
    )(orbitals, noise, potential, *[jnp.asarray(t) for t in tables()], coefs)


def to_rows(block):
    vectors = block.shape[0]
    return block.reshape(vectors, 3, ROWS, 128).transpose(1, 2, 0, 3)


def from_rows(block):
    vectors = block.shape[2]
    return block.transpose(2, 0, 1, 3).reshape(vectors, 3, ROWS * 128)


def local(orbitals, sign_vectors, potential, cheb_coefs):
    high = lax.Precision.HIGHEST
    scale_root = math.sqrt(float(NG) ** 3)
    noise = sign_vectors.astype(jnp.float32)
    whole_potential = lax.all_gather(potential, "grid", axis=0, tiled=True)
    gathered = lax.all_gather(orbitals, "band", axis=0, tiled=True)
    partial_margin = jnp.einsum("ipn,spn->is", gathered, noise, precision=high)
    margins = lax.psum(partial_margin, "grid") / scale_root
    correction = jnp.einsum("is,ipn->spn", margins, gathered, precision=high)
    projected = noise - correction / scale_root
    orb_rows, sto_rows = filter_all(
        to_rows(orbitals), to_rows(projected), whole_potential.reshape(NG, ROWS, 128), cheb_coefs
    )
    squares = (jnp.sum(orb_rows * orb_rows, axis=2) + jnp.sum(sto_rows * sto_rows, axis=2)) / 96.0
    squares = squares.reshape(3, NG * NG)
    density = lax.psum_scatter(squares, "band", scatter_dimension=1, tiled=True)
    return (density, margins, from_rows(sto_rows))


def solution(mesh):
    return jax.shard_map(
        local,
        mesh=mesh,
        in_specs=(P("band", "grid", None), P("band", "grid", None), P("grid", None), P()),
        out_specs=(P("grid", "band"), P(None, "band"), P("band", "grid", None)),
        check_vma=False,
    )
```

time: 1160 us -> 408 us (0.35)
  waiting for transfers between devices: 534 us -> 180 us
  blocking collectives: 358 us -> 55.9 us
  Pallas kernels: 0 us -> 127 us
  local copies, waits for them, and re-layouts: 119 us -> 14.5 us
  matrix products: 89.5 us -> 13.9 us
  starting transfers between devices: 35.8 us -> 0.12 us
    all_to_all x7 -> x0, waiting for transfers between devices: 372 us -> none  [the longest x6 317 us: apply_operator(): lax.all_to_all(turned, 'grid', split_axis=1, concat_axis=2, tiled=True)]
    all_to_all x5 -> x0, blocking collectives: 303 us -> none  [apply_operator(): lax.all_to_all(current, 'grid', split_axis=2, concat_axis=1, tiled=True)]
    pallas_call x0 -> x1, Pallas kernels: none -> 127 us  [filter_all(): pl.pallas_call(filter_kernel, out_shape=(jax.ShapeDtypeStruct((3, ROWS, 4...]
    unnamed x2 -> x4, waiting for transfers between devices: 0.03 us -> 96.5 us
    all_to_all x24 -> x0, local copies, waits for them, and re-layouts: 85.6 us -> none  [the longest x12 47 us: apply_operator(): lax.all_to_all(turned, 'grid', split_axis=1, concat_axis=2, tiled=True)]
    dot_general x19 -> x0, matrix products: 78.6 us -> none  [the longest x6 36.1 us: apply_operator(): along_y = jnp.einsum('vpyz,wy->vpwz', current, kinetic, precision=high)]
    psum x1 -> x0, waiting for transfers between devices: 76.9 us -> none  [local(): summed = lax.psum(squares, 'band')]
    all_to_all x7 -> x0, starting transfers between devices: 35.4 us -> none  [the longest x6 30.3 us: apply_operator(): lax.all_to_all(turned, 'grid', split_axis=1, concat_axis=2, tiled=True)]
  transfers between devices with their start and end apart: 9 -> 3, of which waited for: 9 -> 2; matrix products, arithmetic and copies ran while one was open for 2% -> 3% of each run, Pallas kernels for 0% -> 0%
where the time goes in v1:
time: 408 us
  waiting for transfers between devices  180 us (44%)
  Pallas kernels  127 us (31%)
  blocking collectives  55.9 us (14%)
  local copies, waits for them, and re-layouts  14.5 us (4%)
  matrix products  13.9 us (3%)
  between operations  13.8 us (3%)
    pallas_call x1, Pallas kernels, filter_all(): pl.pallas_call(filter_kernel, out_shape=(jax.ShapeDtypeStruct((3, ROWS, 4...  127 us
    unnamed x4, waiting for transfers between devices  96.5 us
    all_gather x1, waiting for transfers between devices, local(): gathered = lax.all_gather(orbitals, 'band', axis=0, tiled=True)  83.8 us
    psum x1, blocking collectives, local(): margins = lax.psum(partial_margin, 'grid') / scale_root  55.9 us
  transfers between devices with their start and end apart: 3, of which 2 were waited for; matrix products, arithmetic and copies ran while one was open for 3% of the time, Pallas kernels for 0%

profile of v1, /device:TPU:2, one launch (start us, length us, event | category | flops | bytes accessed | tf_op | source)
XLA Modules:
  0.0 407.7 jit_solution(10240778265335117067)
XLA Ops:
  7.2 0.0 copy-start.1
  7.2 0.0 all-gather.4.cloned.1.call-start
  7.2 2.2 copy.10
  9.4 0.0 all-gather.4.cloned.1.call-update
  9.4 0.0 all-gather.6.cloned.1.call-start
  9.5 0.7 all-gather.6.cloned.1.call-update
  10.2 0.0 reduce-scatter.4.cloned.1.call-start
  10.2 83.8 %all-gather.4.cloned.1.call-done = f32[32,3,9216]{2,1,0:T(4,128)} async-done(((f32[4,3,9216]{2,1,0:T(4,128)}), f32[32,3,9216]{2,1,0:T(4,128)}) %all-gather.4.cloned.1.call-update) | async-done | bytes 3538960 | tf_op jit(solution)/shard_map/all_gather | solution.py:250
  94.0 7.0 %fusion.7 = f32[32,8]{0,1:T(8,128)S(1)} fusion(f32[32,3,9216]{2,1,0:T(4,128)} %all-gather.4.cloned.1.call-done, s32[8,3,9216]{2,0,1:T(8,128)} %param.8), kind=kOutput, calls=%fused_computation.6 | convolution fusion | flops 85155840 | bytes 4424704 | tf_op jit(solution)/shard_map/ipn,spn->is/dot_general | solution.py:251
  101.0 55.9 %psum.7 = f32[32,8]{0,1:T(8,128)S(1)} all-reduce(f32[32,8]{0,1:T(8,128)S(1)} %fusion.7), channel_id=1, replica_groups=mesh['grid'=32,'band'=8] {'grid'}, use_global_device_ids=true, to_apply=%region_0.0 | all-reduce | flops 256 | bytes 2048 | tf_op jit(solution)/shard_map/psum | solution.py:252
  156.9 0.0 copy-done.1
  156.9 0.0 copy-start.2
  156.9 6.9 %fusion.4.sto_ref = f32[3,72,8,128]{3,2,1,0:T(8,128)} fusion(f32[32,3,9216]{2,1,0:T(4,128)} %all-gather.4.cloned.1.call-done, s32[8,3,9216]{2,0,1:T(8,128)S(1)} %copy-done.1, f32[32,8]{0,1:T(8,128)S(1)} %broadcast_multiply_fusion), kind=kOutput, calls=%fused_computation.5 | convolution fusion | flops 85598208 | bytes 5309440 | tf_op jit(solution)/shard_map/is,ipn->spn/dot_general | solution.py:253
  163.8 0.0 all-gather.6.cloned.1.call-done
  163.8 6.5 %reshape.26.pot_ref = f32[96,72,128]{2,1,0:T(8,128)} reshape(f32[32,3,9216]{2,1,0:T(4,128)} %all-gather.6.cloned.1.call-done) | data formatting | bytes 7077888 | tf_op jit(solution)/shard_map/reshape | solution.py:256
  170.3 0.0 copy-done.2
  170.3 126.5 %shard_map.94 = (f32[3,72,4,128]{3,2,1,0:T(4,128)}, f32[3,72,8,128]{3,2,1,0:T(8,128)}) custom-call(f32[3,72,4,128]{3,2,1,0:T(4,128)} %bitcast.22, f32[3,72,8,128]{3,2,1,0:T(8,128)} %fusion.4.sto_ref, f32[96,72,128]{2,1,0:T(8,128)} %reshape.26.pot_ref, bf16[192,192]{1,0:T(8,128)(2,1)} %constant.16.clone.kx_ref, bf16[192,192]{1,0:T(8,128)(2,1)} %constant.17.clone.ky_ref, ...), custom_call_target="tpu_custom_call" | custom-call | tf_op jit(solution)/shard_map/pallas_call | solution.py:213
  296.8 1.3 multiply_reduce_fusion.1
  298.1 1.4 multiply_reduce_fusion
  299.6 0.0 copy-start
  299.6 3.0 copy.15
  302.6 0.0 reduce-scatter.4.cloned.1.call-update
  302.6 95.8 %reduce-scatter.4.cloned.1.call-done = f32[1152,3]{1,0:T(8,128)} async-done(((f32[9216,3]{1,0:T(8,128)}), f32[1152,3]{1,0:T(8,128)}) %reduce-scatter.4.cloned.1.call-update) | async-done | bytes 13840
  398.4 1.9 copy.14
  400.3 0.0 copy-done
  400.3 0.9 copy.25
  (2 shorter events, 0.0 us)
Async XLA Ops:
  7.2 149.7 %copy-start.1 = (s32[8,3,9216]{2,0,1:T(8,128)S(1)}, s32[8,3,9216]{2,0,1:T(8,128)}, u32[]{:S(2)}) copy-start(s32[8,3,9216]{2,0,1:T(8,128)} %param.8) | copy-start | bytes 2654212
  7.2 86.8 %all-gather.4.cloned.1.call-start = ((), (), s32[]{:S(2)}) async-start(), calls=%async_computation.1 | async-start | bytes 5308416 | tf_op jit(solution)/shard_map/all_gather | solution.py:250
  9.4 154.3 %all-gather.6.cloned.1.call-start = ((), (), s32[]{:S(2)}) async-start(), calls=%async_computation.2 | async-start | bytes 4866048 | tf_op jit(solution)/shard_map/all_gather | solution.py:249
  10.2 388.2 %reduce-scatter.4.cloned.1.call-start = ((), (), s32[]{:S(2)}) async-start(), calls=%async_computation.3 | async-start | bytes 5308416
  156.9 13.4 %copy-start.2 = (f32[32,8]{0,1:T(8,128)}, f32[32,8]{0,1:T(8,128)S(1)}, u32[]{:S(2)}) copy-start(f32[32,8]{0,1:T(8,128)S(1)} %broadcast_multiply_fusion) | copy-start | bytes 3076
  299.6 100.7 %copy-start = (f32[3,72,8,128]{3,2,1,0:T(8,128)S(1)}, f32[3,72,8,128]{3,2,1,0:T(8,128)}, u32[]{:S(2)}) copy-start(f32[3,72,8,128]{3,2,1,0:T(8,128)} %get-tuple-element.6) | copy-start | bytes 2654212
Sparse Core Ops, SparseCore 0:
  11.2 82.7 all-gather.3
  95.9 66.6 all-gather.5
  302.7 95.5 reduce-scatter.3

commit v2 on v0

v2 whole, which is shorter than its diff:
```python
import math

import jax
import jax.numpy as jnp
import ml_dtypes
import numpy as np
from jax import lax
from jax.experimental import pallas as pl
from jax.experimental.pallas import tpu as pltpu
from jax.sharding import PartitionSpec as P

NG = 96
ORDER = 6
ROWS = 72
XS = 104
UX, UY, UR = 24, 6, 8
BANDS = 8
CHUNK = ROWS // BANDS
SCALE = math.sqrt(float(NG) ** 3)
MESH = pl.DeviceIdType.MESH
ORB_OWNER = tuple(8 * i + 2 * (1 - i % 2) for i in range(4))
STO_OWNER = tuple(4 * s + 2 * ((s // 2) % 2) for s in range(8))


def tables():
    index = np.arange(NG)
    phase = 2.0 * np.pi / NG * ((index[:, None] * index[None, :]) % NG)
    hartley = (np.cos(phase) + np.sin(phase)) / math.sqrt(NG)
    wave = np.minimum(index, NG - index) / (NG / 2.0)
    doubled = 2.0 * (hartley @ (((wave * wave - 0.5) / 3.0)[:, None] * hartley))
    high = doubled.astype(ml_dtypes.bfloat16)
    low = (doubled - high.astype(np.float64)).astype(ml_dtypes.bfloat16)

    def left(order):
        h, l = high[order][:, order], low[order][:, order]
        return np.block([[h, h], [l, l]])

    right = np.zeros((256, 256), ml_dtypes.bfloat16)
    for at in (0, 128):
        right[at : at + NG, 0:NG] = high
        right[at : at + NG, 128 : 128 + NG] = low
    y_order = np.array([4 * (q % 24) + q // 24 for q in range(NG)])
    return left(index), left(y_order), right


def halves(t):
    high = t.astype(jnp.bfloat16)
    return high, (t - high.astype(jnp.float32)).astype(jnp.bfloat16)


def left_mul(matrix, a, b):
    right = jnp.concatenate(
        [jnp.concatenate([a[0], b[0]], 1), jnp.concatenate([a[1], b[1]], 1)], 0
    )
    out = jnp.dot(matrix, right, preferred_element_type=jnp.float32)
    out = out[:NG] + out[NG:]
    return out[:, :128], out[:, 128:]


def spread(a, lane):
    zero = jnp.zeros(lane.shape, jnp.float32)
    one = jnp.where(lane < 32, pltpu.roll(a[0], 32, 1), pltpu.roll(a[1], 32, 1))
    two = jnp.where(lane < 64, pltpu.roll(a[1], 64, 1), pltpu.roll(a[2], 64, 1))
    parts = (a[0], one, two, pltpu.roll(a[2], 96, 1))
    return [jnp.where(lane < 96, part, zero) for part in parts]


def pack(b, lane):
    one = pltpu.roll(b[1], 96, 1)
    two = pltpu.roll(b[2], 64, 1)
    return (
        jnp.where(lane < 96, b[0], one),
        jnp.where(lane < 64, one, two),
        jnp.where(lane < 32, two, pltpu.roll(b[3], 32, 1)),
    )


def quarter(x, j):
    return pl.ds(pl.multiple_of(x * XS + 24 * j, 8), 24)


def wait(view, sem):
    pltpu.make_async_copy(view, view, sem).wait()


def remote(src, dst, send, recv, device):
    return pltpu.make_async_remote_copy(
        src_ref=src, dst_ref=dst, send_sem=send, recv_sem=recv, device_id=device, device_id_type=MESH
    )


def concat_rows(ref, p, kind):
    return jnp.concatenate([ref[p, r].astype(jnp.float32).astype(kind) for r in range(CHUNK)], 1)


def against(a, b, contract):
    return lax.dot_general(a, b, (((1,), (contract,)), ((), ())), preferred_element_type=jnp.float32)


def everything(
    orb, sto, potc, kx, ky, wz, coef_ref, sto_out, mar_out, den_out,
    land, landi, T, W, FI, PO, pot1, pot2, a_orb, a_sto, mt, rs, own_sum, gs, own_mar, ms,
    orb_home, a_f, cbuf, c_home, sto_home, sq, sq_in,
    in_sems, pot1_send, pot1_recv, pot2_send, pot2_recv, land_sem, landi_sem,
    ao_send, ao_recv, as_send, as_recv, rs_send, rs_recv, gs_send, gs_recv, ms_send, ms_recv,
    out_send, oh_recv, sh_recv, af_send, af_recv, c_send, c_recv, sq_send, sq_recv,
):
    me = lax.axis_index("grid")
    band = lax.axis_index("band")
    level = me // 4
    seat = me % 4
    f32 = jnp.float32

    barrier = pltpu.get_barrier_semaphore()
    for j in range(1, 32):
        pl.semaphore_signal(barrier, inc=1, device_id={"grid": lax.rem(me + j, 32)}, device_id_type=MESH)
        other = lax.rem(band * 4 + seat + j, 32)
        pl.semaphore_signal(
            barrier, inc=1, device_id={"band": other // 4, "grid": level * 4 + other % 4}, device_id_type=MESH
        )
    pl.semaphore_wait(barrier, 62)

    turned = (level // 2) % 2
    row = seat // 2
    first_core = seat % 2 == 0
    is_sto = jnp.logical_and(first_core, row == turned)
    is_orb = jnp.logical_and(first_core, jnp.logical_and(row != turned, level % 2 == 0))
    is_owner = jnp.logical_or(is_sto, is_orb)

    def share(d):
        return remote(
            potc, pot1.at[pl.ds(pl.multiple_of(32 * level, 32), 32)], pot1_send, pot1_recv,
            {"grid": lax.rem(level + d, 8) * 4 + seat},
        )

    pltpu.make_async_copy(potc, pot1.at[pl.ds(pl.multiple_of(32 * level, 32), 32)], pot1_recv).start()
    for d in range(1, 8):
        share(d).start()

    def to_owner(v):
        if v < 4:
            return remote(
                orb.at[:, :, v, :], land.at[pl.ds(3 * me, 3)], in_sems.at[v], land_sem, {"grid": ORB_OWNER[v]}
            )
        return remote(
            sto.at[:, :, v - 4, :], landi.at[pl.ds(3 * me, 3)], in_sems.at[v], landi_sem, {"grid": STO_OWNER[v - 4]}
        )

    def send_vectors(low, high):
        for v in range(low, high):
            target = (ORB_OWNER + STO_OWNER)[v]

            @pl.when(me != target)
            def _():
                to_owner(v).start()

            @pl.when(me == target)
            def _():
                if v < 4:
                    pltpu.make_async_copy(orb.at[:, :, v, :], land.at[pl.ds(3 * me, 3)], land_sem).start()
                else:
                    pltpu.make_async_copy(sto.at[:, :, v - 4, :], landi.at[pl.ds(3 * me, 3)], landi_sem).start()

    send_vectors(0, 4)

    wait(pot1, pot1_recv)
    place = pot2.at[pl.ds(pl.multiple_of(256 * (band * 4 + seat), 256), 256)]

    def to_level(kind, d):
        seat_to = 2 * turned if kind == 0 else 2 * (1 - turned)
        return remote(
            pot1, place, pot2_send.at[8 * kind + d], pot2_recv,
            {"band": lax.rem(band + d, BANDS), "grid": level * 4 + seat_to},
        )

    def goes(kind, d):
        go = seat != (2 * turned if kind == 0 else 2 * (1 - turned)) if d == 0 else seat >= 0
        return jnp.logical_and(go, level % 2 == 0) if kind == 1 else go

    for d in range(8):
        for kind in range(2):
            @pl.when(goes(kind, d))
            def _():
                to_level(kind, d).start()

    @pl.when(is_owner)
    def _():
        pltpu.make_async_copy(pot1, place, pot2_recv).start()

    send_vectors(4, 12)

    def cells(src, dst, count, to, sends, recvs):
        return remote(
            src.at[:, pl.ds(CHUNK * to, CHUNK)], dst.at[:, :, pl.ds(pl.multiple_of(count * band, count), count), :],
            sends, recvs, {"band": to},
        )

    def own_cells(src, dst, count, recvs):
        pltpu.make_async_copy(
            src.at[:, pl.ds(CHUNK * band, CHUNK)],
            dst.at[:, :, pl.ds(pl.multiple_of(count * band, count), count), :], recvs,
        ).start()

    own_cells(orb, a_orb, 4, ao_recv)
    own_cells(sto, a_sto, 8, as_recv)
    for d in range(1, 8):
        to = lax.rem(band + d, BANDS)
        cells(orb, a_orb, 4, to, ao_send, ao_recv).start()
        cells(sto, a_sto, 8, to, as_send, as_recv).start()

    def eight(ref, at):
        return ref.at[pl.ds(pl.multiple_of(8 * at, 8), 8)]

    def service_partial():
        wait(a_orb, ao_recv)
        wait(a_sto, as_recv)
        total = jnp.zeros((64, 32), f32)
        for p in range(3):
            signs = concat_rows(a_sto, p, jnp.bfloat16)
            for part in halves(concat_rows(a_orb, p, f32)):
                total += against(signs, part, 1)
        mt[...] = jnp.zeros((64, 128), f32)
        mt[:, 0:32] = total
        pltpu.make_async_copy(eight(mt, band), eight(rs, band), rs_recv).start()
        for d in range(1, 8):
            to = lax.rem(band + d, BANDS)
            remote(eight(mt, to), eight(rs, band), rs_send, rs_recv, {"band": to}).start()

    def service_slab():
        wait(rs, rs_recv)
        own_sum[...] = sum(rs[8 * j : 8 * j + 8, :] for j in range(8))
        pltpu.make_async_copy(own_sum, eight(gs, me), gs_recv).start()

        @pl.loop(1, 32)
        def _(d):
            remote(own_sum, eight(gs, me), gs_send, gs_recv, {"grid": lax.rem(me + d, 32)}).start()

    def service_whole():
        wait(gs, gs_recv)
        margins = sum(gs[8 * j : 8 * j + 8, :] for j in range(32)) / SCALE
        own_mar[...] = margins
        mar_out[...] = margins
        pltpu.make_async_copy(own_mar, eight(ms, band), ms_recv).start()
        for d in range(1, 8):
            remote(own_mar, eight(ms, band), ms_send, ms_recv, {"band": lax.rem(band + d, BANDS)}).start()

    services = (service_partial, service_slab, service_whole)

    @pl.when(jnp.logical_not(is_owner))
    def _():
        for service in services:
            service()

    @pl.when(is_owner)
    def _():
        small = lax.broadcasted_iota(jnp.int32, (8, 128), 1)
        wait(pot2, pot2_recv)

        @pl.loop(0, 32)
        def _(q):
            for p in range(3):
                for m in range(3):
                    parts = spread([pot2[pl.ds(q * 256 + p * 9 + 3 * m + k, 8, stride=32), :] for k in range(3)], small)
                    for j, part in enumerate(parts):
                        at = (3 * (q % 4) + p) * XS + 24 * j + 3 * (q // 4) + m
                        PO[pl.ds(at, 8, stride=12 * XS), :] = 2.0 * part

        lane = lax.broadcasted_iota(jnp.int32, (24, 128), 1)
        first_coef = coef_ref[0]

        def take(source):
            @pl.loop(0, NG, step=UR)
            def _(base):
                for u in range(UR):
                    x = base + u
                    rows = [source[x, pl.ds(k, 24, stride=3), :].astype(f32) for k in range(3)]
                    for j, part in enumerate(spread(rows, lane)):
                        T[0, quarter(x, j), :] = part
                        FI[quarter(x, j), :] = first_coef * part

        @pl.when(is_orb)
        def _():
            wait(land, land_sem)
            take(land)

        @pl.when(is_sto)
        def _():
            wait(landi, landi_sem)
            take(landi)

        @pl.loop(0, ORDER)
        def _(k):
            for at, service in enumerate(services):
                @pl.when(k == 2 + at)
                def _():
                    service()

            apply_operator(k, kx, ky, wz, coef_ref, T, W, FI, PO)

        @pl.loop(0, NG, step=UR)
        def _(base):
            for u in range(UR):
                x = base + u
                for k, part in enumerate(pack([FI[quarter(x, j), :] for j in range(4)], lane)):
                    land[x, pl.ds(k, 24, stride=3), :] = part

    def hand_back(home, at, recv):
        pltpu.make_async_copy(land.at[pl.ds(3 * me, 3)], home.at[:, :, at, :], recv).start()

        @pl.loop(1, 32)
        def _(d):
            to = lax.rem(me + d, 32)
            remote(land.at[pl.ds(3 * to, 3)], home.at[:, :, at, :], out_send, recv, {"grid": to}).start()

    for v, target in enumerate(ORB_OWNER + STO_OWNER):
        @pl.when(me == target)
        def _():
            hand_back(*((orb_home, v, oh_recv) if v < 4 else (sto_home, v - 4, sh_recv)))

    wait(orb_home, oh_recv)
    own_cells(orb_home, a_f, 4, af_recv)
    for d in range(1, 8):
        cells(orb_home, a_f, 4, lax.rem(band + d, BANDS), af_send, af_recv).start()
    wait(ms, ms_recv)
    m_high, m_low = halves(ms[:, 0:32] * (1.0 / SCALE))
    wait(a_f, af_recv)
    orb_squares = []
    for p in range(3):
        field = concat_rows(a_f, p, f32)
        f_high, f_low = halves(field)
        change = against(m_high, f_high, 0) + against(m_high, f_low, 0) + against(m_low, f_high, 0)
        summed = jnp.sum(field * field, axis=0, keepdims=True)
        for r in range(CHUNK):
            cbuf[p, r] = change[:, 128 * r : 128 * r + 128]
            orb_squares.append(summed[:, 128 * r : 128 * r + 128])

    def back(to):
        return remote(
            cbuf.at[:, :, pl.ds(pl.multiple_of(8 * to, 8), 8), :], c_home.at[:, pl.ds(CHUNK * band, CHUNK)],
            c_send, c_recv, {"band": to},
        )

    pltpu.make_async_copy(
        cbuf.at[:, :, pl.ds(pl.multiple_of(8 * band, 8), 8), :], c_home.at[:, pl.ds(CHUNK * band, CHUNK)], c_recv
    ).start()
    for d in range(1, 8):
        back(lax.rem(band + d, BANDS)).start()

    wait(c_home, c_recv)
    wait(sto_home, sh_recv)

    @pl.loop(0, BANDS)
    def _(b):
        for p in range(3):
            for r in range(CHUNK):
                at = b * CHUNK + r
                value = sto_home[p, at] - c_home[p, at]
                sto_out[p, at] = value
                sq[b, pl.ds(p * CHUNK + r, 1), :] = jnp.sum(value * value, axis=0, keepdims=True)

    pltpu.make_async_copy(sq.at[band], sq_in.at[band], sq_recv).start()
    for d in range(1, 8):
        to = lax.rem(band + d, BANDS)
        remote(sq.at[to], sq_in.at[band], sq_send, sq_recv, {"band": to}).start()
    wait(sq_in, sq_recv)
    for at, orbital_part in enumerate(orb_squares):
        den_out[at : at + 1, :] = orbital_part
    den_out[...] = (den_out[...] + sum(sq_in[b] for b in range(BANDS))) / 96.0

    wait(pot1.at[pl.ds(0, 224)], pot1_send)
    for d in range(8):
        for kind in range(2):
            @pl.when(goes(kind, d))
            def _():
                to_level(kind, d).wait_send()
    for v, target in enumerate(ORB_OWNER + STO_OWNER):
        @pl.when(me != target)
        def _():
            to_owner(v).wait_send()
    wait(orb.at[:, pl.ds(0, 7 * CHUNK)], ao_send)
    wait(sto.at[:, pl.ds(0, 7 * CHUNK)], as_send)
    wait(rs.at[pl.ds(0, 56)], rs_send)
    wait(gs.at[pl.ds(0, 248)], gs_send)
    wait(ms.at[pl.ds(0, 56)], ms_send)

    @pl.when(is_owner)
    def _():
        wait(land.at[pl.ds(0, 93)], out_send)

    wait(orb_home.at[:, pl.ds(0, 7 * CHUNK)], af_send)
    wait(c_home.at[:, pl.ds(0, 7 * CHUNK)], c_send)
    wait(sq.at[pl.ds(0, 7)], sq_send)


def apply_operator(k, kx_ref, ky_ref, wz_ref, coef_ref, T, W, FI, PO):
    now = lax.rem(k, 2)
    other = 1 - now
    alpha = jnp.where(k == 0, 0.5, 1.0)
    beta = jnp.where(k == 0, 0.0, 1.0)
    coef = coef_ref[k + 1]

    @pl.loop(0, NG, step=2 * UX)
    def _(base):
        for u in range(UX):
            y = base + 2 * u
            columns = [pl.ds(y + q, NG, stride=XS) for q in range(2)]
            outs = left_mul(kx_ref[...], *[halves(T[now, c, :]) for c in columns])
            for c, out in zip(columns, outs):
                W[c, :] = out

    @pl.loop(0, NG, step=2 * UY)
    def _(base):
        rows = [pl.ds(pl.multiple_of((base + q) * XS, 8), NG) for q in range(2 * UY)]
        held = [T[now, r, :] for r in rows]
        split = [halves(t) for t in held]
        along_y = []
        for u in range(UY):
            along_y += left_mul(ky_ref[...], split[2 * u], split[2 * u + 1])
        stacked = jnp.concatenate([jnp.concatenate(pair, 1) for pair in split], 0)
        along_z = jnp.dot(stacked, wz_ref[...], preferred_element_type=jnp.float32)
        for q, r in enumerate(rows):
            z = along_z[NG * q : NG * (q + 1)]
            total = z[:, :128] + z[:, 128:] + along_y[q] + W[r, :] + PO[r, :] * held[q]
            following = alpha * total - beta * T[other, r, :]
            T[other, r, :] = following
            FI[r, :] = FI[r, :] + coef * following


def to_rows(block):
    vectors = block.shape[0]
    return block.reshape(vectors, 3, ROWS, 128).transpose(1, 2, 0, 3)


def from_rows(block):
    vectors = block.shape[2]
    return block.transpose(2, 0, 1, 3).reshape(vectors, 3, ROWS * 128)


def local(orbitals, sign_vectors, potential, cheb_coefs):
    f32 = jnp.float32
    vmem = pl.BlockSpec(memory_space=pltpu.VMEM)
    anywhere = pl.BlockSpec(memory_space=pl.ANY)
    share = lax.dynamic_slice_in_dim(potential, lax.axis_index("band") * (CHUNK * 128), CHUNK * 128, 1)
    share = jnp.pad(share.reshape(3 * CHUNK, 128), ((0, 5), (0, 0)))
    field = pltpu.VMEM((NG * XS, 128), f32)
    dma = pltpu.SemaphoreType.DMA
    noise, margins, density = pl.pallas_call(
        everything,
        out_shape=(
            jax.ShapeDtypeStruct((3, ROWS, 8, 128), f32),
            jax.ShapeDtypeStruct((8, 128), f32),
            jax.ShapeDtypeStruct((3 * CHUNK, 128), f32),
        ),
        in_specs=[anywhere, anywhere] + [vmem] * 4 + [pl.BlockSpec(memory_space=pltpu.SMEM)],
        out_specs=(vmem, vmem, vmem),
        scratch_shapes=[
            pltpu.VMEM((NG, ROWS, 128), f32),
            pltpu.VMEM((NG, ROWS, 128), jnp.int32),
            pltpu.VMEM((2, NG * XS, 128), f32),
            field, field, field,
            pltpu.VMEM((256, 128), f32),
            pltpu.VMEM((8192, 128), f32),
            pltpu.VMEM((3, CHUNK, 32, 128), f32),
            pltpu.VMEM((3, CHUNK, 64, 128), jnp.int32),
            pltpu.VMEM((64, 128), f32),
            pltpu.VMEM((64, 128), f32),
            pltpu.VMEM((8, 128), f32),
            pltpu.VMEM((256, 128), f32),
            pltpu.VMEM((8, 128), f32),
            pltpu.VMEM((64, 128), f32),
            pltpu.VMEM((3, ROWS, 4, 128), f32),
            pltpu.VMEM((3, CHUNK, 32, 128), f32),
            pltpu.VMEM((3, CHUNK, 64, 128), f32),
            pltpu.VMEM((3, ROWS, 8, 128), f32),
            pltpu.VMEM((3, ROWS, 8, 128), f32),
            pltpu.VMEM((BANDS, 3 * CHUNK, 128), f32),
            pltpu.VMEM((BANDS, 3 * CHUNK, 128), f32),
            dma((12,)), dma, dma, dma((16,)), dma, dma, dma,
            dma, dma, dma, dma, dma, dma, dma, dma, dma, dma,
            dma, dma, dma, dma, dma, dma, dma, dma, dma,
        ],
        compiler_params=pltpu.CompilerParams(
            vmem_limit_bytes=60 * 2**20, has_side_effects=True, collective_id=1
        ),
    )(
        to_rows(orbitals), to_rows(sign_vectors), share,
        *[jnp.asarray(t) for t in tables()], cheb_coefs,
    )
    return density.reshape(3, CHUNK * 128), margins[:, :32].T, from_rows(noise)


def solution(mesh):
    return jax.shard_map(
        local,
        mesh=mesh,
        in_specs=(P("band", "grid", None), P("band", "grid", None), P("grid", None), P()),
        out_specs=(P("grid", "band"), P(None, "band"), P("band", "grid", None)),
        check_vma=False,
    )
```

time: 1160 us -> 199 us (0.17)
  waiting for transfers between devices: 534 us -> 0 us
  blocking collectives: 358 us -> 0 us
  Pallas kernels: 0 us -> 189 us
  local copies, waits for them, and re-layouts: 119 us -> 5.6 us
  matrix products: 89.5 us -> 0 us
  starting transfers between devices: 35.8 us -> 0 us
  between operations: 14.9 us -> 0.66 us
    all_to_all x7 -> x0, waiting for transfers between devices: 372 us -> none  [the longest x6 317 us: apply_operator(): lax.all_to_all(turned, 'grid', split_axis=1, concat_axis=2, tiled=True)]
    all_to_all x5 -> x0, blocking collectives: 303 us -> none  [apply_operator(): lax.all_to_all(current, 'grid', split_axis=2, concat_axis=1, tiled=True)]
    pallas_call x0 -> x1, Pallas kernels: none -> 189 us  [local(): pl.pallas_call(everything, out_shape=(jax.ShapeDtypeStruct((3, ROWS, 8, 1...]
    dot_general x21 -> x0, matrix products: 89.5 us -> none  [the longest x6 36.1 us: apply_operator(): along_y = jnp.einsum('vpyz,wy->vpwz', current, kinetic, precision=high)]
    all_to_all x24 -> x0, local copies, waits for them, and re-layouts: 85.6 us -> none  [the longest x12 47 us: apply_operator(): lax.all_to_all(turned, 'grid', split_axis=1, concat_axis=2, tiled=True)]
    all_gather x1 -> x0, waiting for transfers between devices: 84.6 us -> none  [local(): gathered = lax.all_gather(orbitals, 'band', axis=0, tiled=True)]
    psum x1 -> x0, waiting for transfers between devices: 76.9 us -> none  [local(): summed = lax.psum(squares, 'band')]
    psum x1 -> x0, blocking collectives: 55.4 us -> none  [local(): margins = lax.psum(partial_margin, 'grid') / scale_root]
  transfers between devices with their start and end apart: 9 -> 0, of which waited for: 9 -> 0; matrix products, arithmetic and copies ran while one was open for 2% -> 0% of each run, Pallas kernels for 0% -> 0%
where the time goes in v2:
time: 199 us; the launch traced here: 195 us
  Pallas kernels  189 us (95%)
  local copies, waits for them, and re-layouts  5.6 us (3%)
    pallas_call x1, Pallas kernels, local(): pl.pallas_call(everything, out_shape=(jax.ShapeDtypeStruct((3, ROWS, 8, 1...  189 us

profile of v2, /device:TPU:2, one launch (start us, length us, event | category | flops | bytes accessed | tf_op | source)
XLA Modules:
  0.0 195.4 jit_solution(3901725872960893619)
XLA Ops:
  0.6 0.0 copy-start
  0.6 0.9 copy-done
  1.6 0.6 pad.4.potc
  2.2 189.1 %shard_map.94 = (f32[3,72,8,128]{3,2,1,0:T(8,128)}, f32[8,128]{1,0:T(8,128)}, f32[27,128]{1,0:T(8,128)}) custom-call(f32[3,72,4,128]{3,2,1,0:T(4,128)} %bitcast.13, s32[3,72,8,128]{3,2,1,0:T(8,128)} %bitcast.11, f32[32,128]{1,0:T(8,128)} %pad.4.potc, bf16[192,192]{1,0:T(8,128)(2,1)} %constant.18.clone.kx, bf16[192,192]{1,0:T(8,128)(2,1)} %constant.19.clone.ky, ...), custom_call_target="tpu_custom_call" | custom-call | tf_op jit(solution)/shard_map/pallas_call | solution.py:447
  191.3 0.0 copy-start.1
  191.3 1.3 reshape.24
  192.7 0.0 copy-done.1
  192.7 0.6 slice_bitcast_fusion
  193.3 2.1 %copy.11 = f32[8,3,9216]{2,0,1:T(8,128)} copy(f32[8,3,9216]{2,0,1:T(8,128)} %bitcast.12) | data formatting | bytes 1769472
  (2 shorter events, 0.0 us)
Async XLA Ops:
  0.6 0.9 copy-start
  191.3 1.3 copy-start.1

commit v3 on v2

--- a/solution.py
+++ b/solution.py
@@ -13,7 +13,9 @@
 ORDER = 6
 ROWS = 72
 XS = 104
-UX, UY, UR = 24, 6, 8
+UX, UY, UR = 24, 12, 8
+SHARE = 56
+BLOCK = 16 * SHARE
 BANDS = 8
 CHUNK = ROWS // BANDS
 SCALE = math.sqrt(float(NG) ** 3)
@@ -99,9 +101,9 @@
 
 def everything(
     orb, sto, potc, kx, ky, wz, coef_ref, sto_out, mar_out, den_out,
-    land, landi, T, W, FI, PO, pot1, pot2, a_orb, a_sto, mt, rs, own_sum, gs, own_mar, ms,
+    land, landi, T, W, FI, PO, pot2, a_orb, a_sto, mt, rs, own_sum, gs, own_mar, ms,
     orb_home, a_f, cbuf, c_home, sto_home, sq, sq_in,
-    in_sems, pot1_send, pot1_recv, pot2_send, pot2_recv, land_sem, landi_sem,
+    in_sems, pot1_send, pot1_recv, pot2_send, pot2_recv, pot3_send, pot3_recv, land_sem, landi_sem,
     ao_send, ao_recv, as_send, as_recv, rs_send, rs_recv, gs_send, gs_recv, ms_send, ms_recv,
     out_send, oh_recv, sh_recv, af_send, af_recv, c_send, c_recv, sq_send, sq_recv,
 ):
@@ -114,28 +116,46 @@
     barrier = pltpu.get_barrier_semaphore()
     for j in range(1, 32):
         pl.semaphore_signal(barrier, inc=1, device_id={"grid": lax.rem(me + j, 32)}, device_id_type=MESH)
-        other = lax.rem(band * 4 + seat + j, 32)
-        pl.semaphore_signal(
-            barrier, inc=1, device_id={"band": other // 4, "grid": level * 4 + other % 4}, device_id_type=MESH
-        )
-    pl.semaphore_wait(barrier, 62)
+    for j in range(1, BANDS):
+        pl.semaphore_signal(barrier, inc=1, device_id={"band": lax.rem(band + j, BANDS)}, device_id_type=MESH)
+    pl.semaphore_wait(barrier, 38)
 
     turned = (level // 2) % 2
     row = seat // 2
-    first_core = seat % 2 == 0
-    is_sto = jnp.logical_and(first_core, row == turned)
-    is_orb = jnp.logical_and(first_core, jnp.logical_and(row != turned, level % 2 == 0))
+    core = seat % 2
+    column = band % 4
+    is_chip = jnp.logical_or(row == turned, level % 2 == 0)
+    is_sto = jnp.logical_and(core == 0, row == turned)
+    is_orb = jnp.logical_and(core == 0, jnp.logical_and(row != turned, level % 2 == 0))
     is_owner = jnp.logical_or(is_sto, is_orb)
 
-    def share(d):
+    def block(a_core, a_column, blocks=1):
+        return pot2.at[pl.ds(pl.multiple_of(BLOCK * (4 * a_core + a_column), 8), BLOCK * blocks)]
+
+    slot = pot2.at[pl.ds(pl.multiple_of(BLOCK * (4 * core + column) + SHARE * (2 * level + row), 8), SHARE)]
+
+    def share(kind, d):
+        there = lax.rem(level + d, 8)
+        row_to = (there // 2 + kind) % 2
         return remote(
-            potc, pot1.at[pl.ds(pl.multiple_of(32 * level, 32), 32)], pot1_send, pot1_recv,
-            {"grid": lax.rem(level + d, 8) * 4 + seat},
+            potc, slot, pot1_send.at[8 * kind + d], pot1_recv, {"grid": there * 4 + 2 * row_to + core}
         )
 
-    pltpu.make_async_copy(potc, pot1.at[pl.ds(pl.multiple_of(32 * level, 32), 32)], pot1_recv).start()
-    for d in range(1, 8):
-        share(d).start()
+    def shares(kind, d):
+        go = level >= 0 if kind == 0 else (level + d) % 2 == 0
+        if d == 0:
+            go = jnp.logical_and(go, row != turned if kind == 0 else row == turned)
+        return go
+
+    @pl.when(is_chip)
+    def _():
+        pltpu.make_async_copy(potc, slot, pot1_recv).start()
+
+    for d in range(8):
+        for kind in range(2):
+            @pl.when(shares(kind, d))
+            def _():
+                share(kind, d).start()
 
     def to_owner(v):
         if v < 4:
@@ -163,31 +183,37 @@
 
     send_vectors(0, 4)
 
-    wait(pot1, pot1_recv)
-    place = pot2.at[pl.ds(pl.multiple_of(256 * (band * 4 + seat), 256), 256)]
-
-    def to_level(kind, d):
-        seat_to = 2 * turned if kind == 0 else 2 * (1 - turned)
+    def along(d):
         return remote(
-            pot1, place, pot2_send.at[8 * kind + d], pot2_recv,
-            {"band": lax.rem(band + d, BANDS), "grid": level * 4 + seat_to},
+            block(core, column), block(core, column), pot2_send, pot2_recv,
+            {"band": (band // 4) * 4 + lax.rem(column + d, 4)},
         )
 
-    def goes(kind, d):
-        go = seat != (2 * turned if kind == 0 else 2 * (1 - turned)) if d == 0 else seat >= 0
-        return jnp.logical_and(go, level % 2 == 0) if kind == 1 else go
-
-    for d in range(8):
-        for kind in range(2):
-            @pl.when(goes(kind, d))
-            def _():
-                to_level(kind, d).start()
-
-    @pl.when(is_owner)
-    def _():
-        pltpu.make_async_copy(pot1, place, pot2_recv).start()
+    @pl.when(is_chip)
+    def _():
+        wait(block(core, column), pot1_recv)
+        for d in range(1, 4):
+            along(d).start()
 
     send_vectors(4, 12)
+
+    across = remote(
+        block(1, 0, 4), block(1, 0, 4), pot3_send, pot3_recv, {"grid": level * 4 + 2 * row}
+    )
+    hands_over = jnp.logical_and(is_chip, core == 1)
+
+    @pl.when(is_chip)
+    def _():
+        wait(block(0, 0, 3), pot2_recv)
+
+        @pl.when(hands_over)
+        def _():
+            across.start()
+
+    for v, target in enumerate(ORB_OWNER + STO_OWNER):
+        @pl.when(me != target)
+        def _():
+            to_owner(v).wait_send()
 
     def cells(src, dst, count, to, sends, recvs):
         return remote(
@@ -253,20 +279,23 @@
 
     @pl.when(is_owner)
     def _():
-        small = lax.broadcasted_iota(jnp.int32, (8, 128), 1)
-        wait(pot2, pot2_recv)
-
-        @pl.loop(0, 32)
+        wait(block(0, 0, 4), pot3_recv)
+        small = lax.broadcasted_iota(jnp.int32, (16, 128), 1)
+
+        @pl.loop(0, 8)
         def _(q):
             for p in range(3):
-                for m in range(3):
-                    parts = spread([pot2[pl.ds(q * 256 + p * 9 + 3 * m + k, 8, stride=32), :] for k in range(3)], small)
+                for m in range(6):
+                    parts = spread(
+                        [pot2[pl.ds(q * BLOCK + p * 18 + 3 * m + k, 16, stride=SHARE), :] for k in range(3)], small
+                    )
                     for j, part in enumerate(parts):
-                        at = (3 * (q % 4) + p) * XS + 24 * j + 3 * (q // 4) + m
-                        PO[pl.ds(at, 8, stride=12 * XS), :] = 2.0 * part
+                        at = (3 * (q // 4) + p) * XS + 24 * j + 6 * (q % 4) + m
+                        PO[pl.ds(at, 16, stride=6 * XS), :] = 2.0 * part
 
         lane = lax.broadcasted_iota(jnp.int32, (24, 128), 1)
-        first_coef = coef_ref[0]
+
+        last_coef = coef_ref[ORDER]
 
         def take(source):
             @pl.loop(0, NG, step=UR)
@@ -275,8 +304,8 @@
                     x = base + u
                     rows = [source[x, pl.ds(k, 24, stride=3), :].astype(f32) for k in range(3)]
                     for j, part in enumerate(spread(rows, lane)):
-                        T[0, quarter(x, j), :] = part
-                        FI[quarter(x, j), :] = first_coef * part
+                        T[0, quarter(x, j), :] = last_coef * part
+                        FI[quarter(x, j), :] = part
 
         @pl.when(is_orb)
         def _():
@@ -288,34 +317,45 @@
             wait(landi, landi_sem)
             take(landi)
 
-        @pl.loop(0, ORDER)
+        fields = (kx, ky, wz, coef_ref, T, W, FI, PO)
+        apply_operator(0, 0, 1, UY, None, *fields)
+
+        @pl.loop(1, ORDER - 1)
         def _(k):
-            for at, service in enumerate(services):
-                @pl.when(k == 2 + at)
+            for at, service in enumerate(services[:2]):
+                @pl.when(jnp.logical_and(is_sto, k == 3 + at))
                 def _():
                     service()
 
-            apply_operator(k, kx, ky, wz, coef_ref, T, W, FI, PO)
-
-        @pl.loop(0, NG, step=UR)
-        def _(base):
-            for u in range(UR):
+            apply_operator(k, lax.rem(k, 2), 1 - lax.rem(k, 2), UY, None, *fields)
+
+        def hand_back(base):
+            for u in range(12):
                 x = base + u
                 for k, part in enumerate(pack([FI[quarter(x, j), :] for j in range(4)], lane)):
                     land[x, pl.ds(k, 24, stride=3), :] = part
-
-    def hand_back(home, at, recv):
-        pltpu.make_async_copy(land.at[pl.ds(3 * me, 3)], home.at[:, :, at, :], recv).start()
-
-        @pl.loop(1, 32)
-        def _(d):
-            to = lax.rem(me + d, 32)
-            remote(land.at[pl.ds(3 * to, 3)], home.at[:, :, at, :], out_send, recv, {"grid": to}).start()
-
-    for v, target in enumerate(ORB_OWNER + STO_OWNER):
-        @pl.when(me == target)
+            for u in range(4):
+                to = base // 3 + u
+                slab = land.at[pl.ds(3 * to, 3)]
+                for kind, home, at, recv in (
+                    (is_orb, orb_home, level // 2, oh_recv), (is_sto, sto_home, level, sh_recv)
+                ):
+                    @pl.when(jnp.logical_and(kind, to != me))
+                    def _():
+                        remote(slab, home.at[:, :, at, :], out_send, recv, {"grid": to}).start()
+
+                    @pl.when(jnp.logical_and(kind, to == me))
+                    def _():
+                        pltpu.make_async_copy(slab, home.at[:, :, at, :], recv).start()
+
+        apply_operator(ORDER - 1, 1, 0, 6, hand_back, *fields)
+
+        @pl.when(is_orb)
         def _():
-            hand_back(*((orb_home, v, oh_recv) if v < 4 else (sto_home, v - 4, sh_recv)))
+            service_partial()
+            service_slab()
+
+        service_whole()
 
     wait(orb_home, oh_recv)
     own_cells(orb_home, a_f, 4, af_recv)
@@ -363,20 +403,26 @@
         to = lax.rem(band + d, BANDS)
         remote(sq.at[to], sq_in.at[band], sq_send, sq_recv, {"band": to}).start()
     wait(sq_in, sq_recv)
-    for at, orbital_part in enumerate(orb_squares):
-        den_out[at : at + 1, :] = orbital_part
-    den_out[...] = (den_out[...] + sum(sq_in[b] for b in range(BANDS))) / 96.0
-
-    wait(pot1.at[pl.ds(0, 224)], pot1_send)
+    noise_part = sum(sq_in[b] for b in range(BANDS))
+    for p in range(3):
+        for r in range(CHUNK):
+            at = p * CHUNK + r
+            den_out[p : p + 1, 128 * r : 128 * r + 128] = (orb_squares[at] + noise_part[at : at + 1]) / 96.0
+
     for d in range(8):
         for kind in range(2):
-            @pl.when(goes(kind, d))
+            @pl.when(shares(kind, d))
             def _():
-                to_level(kind, d).wait_send()
-    for v, target in enumerate(ORB_OWNER + STO_OWNER):
-        @pl.when(me != target)
+                share(kind, d).wait_send()
+
+    @pl.when(is_chip)
+    def _():
+        wait(block(0, 0, 3), pot2_send)
+
+        @pl.when(hands_over)
         def _():
-            to_owner(v).wait_send()
+            across.wait_send()
+
     wait(orb.at[:, pl.ds(0, 7 * CHUNK)], ao_send)
     wait(sto.at[:, pl.ds(0, 7 * CHUNK)], as_send)
     wait(rs.at[pl.ds(0, 56)], rs_send)
@@ -392,12 +438,8 @@
     wait(sq.at[pl.ds(0, 7)], sq_send)
 
 
-def apply_operator(k, kx_ref, ky_ref, wz_ref, coef_ref, T, W, FI, PO):
-    now = lax.rem(k, 2)
-    other = 1 - now
-    alpha = jnp.where(k == 0, 0.5, 1.0)
-    beta = jnp.where(k == 0, 0.0, 1.0)
-    coef = coef_ref[k + 1]
+def apply_operator(k, now, other, group, emit, kx_ref, ky_ref, wz_ref, coef_ref, T, W, FI, PO):
+    coef = coef_ref[ORDER - 1 - k]
 
     @pl.loop(0, NG, step=2 * UX)
     def _(base):
@@ -408,22 +450,28 @@
             for c, out in zip(columns, outs):
                 W[c, :] = out
 
-    @pl.loop(0, NG, step=2 * UY)
+    @pl.loop(0, NG, step=2 * group)
     def _(base):
-        rows = [pl.ds(pl.multiple_of((base + q) * XS, 8), NG) for q in range(2 * UY)]
+        rows = [pl.ds(pl.multiple_of((base + q) * XS, 8), NG) for q in range(2 * group)]
         held = [T[now, r, :] for r in rows]
         split = [halves(t) for t in held]
-        along_y = []
-        for u in range(UY):
-            along_y += left_mul(ky_ref[...], split[2 * u], split[2 * u + 1])
-        stacked = jnp.concatenate([jnp.concatenate(pair, 1) for pair in split], 0)
-        along_z = jnp.dot(stacked, wz_ref[...], preferred_element_type=jnp.float32)
-        for q, r in enumerate(rows):
-            z = along_z[NG * q : NG * (q + 1)]
-            total = z[:, :128] + z[:, 128:] + along_y[q] + W[r, :] + PO[r, :] * held[q]
-            following = alpha * total - beta * T[other, r, :]
-            T[other, r, :] = following
-            FI[r, :] = FI[r, :] + coef * following
+        for u in range(group):
+            along_y = left_mul(ky_ref[...], split[2 * u], split[2 * u + 1])
+            stacked = jnp.concatenate([jnp.concatenate(split[2 * u + q], 1) for q in range(2)], 0)
+            along_z = jnp.dot(stacked, wz_ref[...], preferred_element_type=jnp.float32)
+            for q in range(2):
+                r = rows[2 * u + q]
+                t = held[2 * u + q]
+                z = along_z[NG * q : NG * (q + 1)]
+                total = z[:, :128] + z[:, 128:] + along_y[q] + W[r, :] + PO[r, :] * t
+                if emit is not None:
+                    FI[r, :] = coef * FI[r, :] + 0.5 * total - T[other, r, :]
+                elif isinstance(k, int):
+                    T[other, r, :] = coef * FI[r, :] + total
+                else:
+                    T[other, r, :] = coef * FI[r, :] + total - T[other, r, :]
+        if emit is not None:
+            emit(base)
 
 
 def to_rows(block):
@@ -440,8 +488,11 @@
     f32 = jnp.float32
     vmem = pl.BlockSpec(memory_space=pltpu.VMEM)
     anywhere = pl.BlockSpec(memory_space=pl.ANY)
-    share = lax.dynamic_slice_in_dim(potential, lax.axis_index("band") * (CHUNK * 128), CHUNK * 128, 1)
-    share = jnp.pad(share.reshape(3 * CHUNK, 128), ((0, 5), (0, 0)))
+    quarter_lanes = 18 * 128
+    share = lax.dynamic_slice_in_dim(
+        potential, (lax.axis_index("band") % 4) * quarter_lanes, quarter_lanes, 1
+    )
+    share = jnp.pad(share.reshape(54, 128), ((0, SHARE - 54), (0, 0)))
     field = pltpu.VMEM((NG * XS, 128), f32)
     dma = pltpu.SemaphoreType.DMA
     noise, margins, density = pl.pallas_call(
@@ -449,7 +500,7 @@
         out_shape=(
             jax.ShapeDtypeStruct((3, ROWS, 8, 128), f32),
             jax.ShapeDtypeStruct((8, 128), f32),
-            jax.ShapeDtypeStruct((3 * CHUNK, 128), f32),
+            jax.ShapeDtypeStruct((3, CHUNK * 128), f32),
         ),
         in_specs=[anywhere, anywhere] + [vmem] * 4 + [pl.BlockSpec(memory_space=pltpu.SMEM)],
         out_specs=(vmem, vmem, vmem),
@@ -458,8 +509,7 @@
             pltpu.VMEM((NG, ROWS, 128), jnp.int32),
             pltpu.VMEM((2, NG * XS, 128), f32),
             field, field, field,
-            pltpu.VMEM((256, 128), f32),
-            pltpu.VMEM((8192, 128), f32),
+            pltpu.VMEM((8 * BLOCK, 128), f32),
             pltpu.VMEM((3, CHUNK, 32, 128), f32),
             pltpu.VMEM((3, CHUNK, 64, 128), jnp.int32),
             pltpu.VMEM((64, 128), f32),
@@ -475,7 +525,7 @@
             pltpu.VMEM((3, ROWS, 8, 128), f32),
             pltpu.VMEM((BANDS, 3 * CHUNK, 128), f32),
             pltpu.VMEM((BANDS, 3 * CHUNK, 128), f32),
-            dma((12,)), dma, dma, dma((16,)), dma, dma, dma,
+            dma((12,)), dma((16,)), dma, dma, dma, dma, dma, dma, dma,
             dma, dma, dma, dma, dma, dma, dma, dma, dma, dma,
             dma, dma, dma, dma, dma, dma, dma, dma, dma,
         ],
@@ -486,7 +536,7 @@
         to_rows(orbitals), to_rows(sign_vectors), share,
         *[jnp.asarray(t) for t in tables()], cheb_coefs,
     )
-    return density.reshape(3, CHUNK * 128), margins[:, :32].T, from_rows(noise)
+    return density, margins[:, :32].T, from_rows(noise)
 
 
 def solution(mesh):

time: 199 us -> 173 us (0.87)
  Pallas kernels: 189 us -> 164 us
    pallas_call x1, Pallas kernels: 189 us -> 164 us  [local(): pl.pallas_call(everything, out_shape=(jax.ShapeDtypeStruct((3, ROWS, 8, 1...]
    unnamed x5 -> x6, local copies, waits for them, and re-layouts: 3.04 us -> 5.02 us
where the time goes in v3:
time: 173 us; the launch traced here: 171 us
  Pallas kernels  164 us (95%)
  local copies, waits for them, and re-layouts  6.26 us (4%)
    pallas_call x1, Pallas kernels, local(): pl.pallas_call(everything, out_shape=(jax.ShapeDtypeStruct((3, ROWS, 8, 1...  164 us
    unnamed x6, local copies, waits for them, and re-layouts  5.02 us

profile of v3, /device:TPU:2, one launch (start us, length us, event | category | flops | bytes accessed | tf_op | source)
XLA Modules:
  0.0 170.7 jit_solution(17270810553312103847)
XLA Ops:
  0.6 0.0 copy-start
  0.7 0.9 copy-done
  1.6 0.6 pad.4.potc
  2.2 163.8 %shard_map.94 = (f32[3,72,8,128]{3,2,1,0:T(8,128)}, f32[8,128]{1,0:T(8,128)}, f32[3,1152]{1,0:T(4,128)}) custom-call(f32[3,72,4,128]{3,2,1,0:T(4,128)} %bitcast.13, s32[3,72,8,128]{3,2,1,0:T(8,128)} %bitcast.11, f32[56,128]{1,0:T(8,128)} %pad.4.potc, bf16[192,192]{1,0:T(8,128)(2,1)} %constant.30.clone.kx, bf16[192,192]{1,0:T(8,128)(2,1)} %constant.31.clone.ky, ...), custom_call_target="tpu_custom_call" | custom-call | tf_op jit(solution)/shard_map/pallas_call | solution.py:498
  166.0 0.0 copy-start.1
  166.0 0.7 copy-done.1
  166.6 0.6 slice_bitcast_fusion
  167.2 1.3 copy.12
  168.6 2.1 %copy.13 = f32[8,3,9216]{2,0,1:T(8,128)} copy(f32[8,3,9216]{2,0,1:T(8,128)} %bitcast.12) | data formatting | bytes 1769472
  (2 shorter events, 0.0 us)
Async XLA Ops:
  0.6 0.9 copy-start
  166.0 0.7 copy-start.1

commit v4 on v3

--- a/solution.py
+++ b/solution.py
@@ -185,8 +185,16 @@
 
     def along(d):
         return remote(
-            block(core, column), block(core, column), pot2_send, pot2_recv,
+            block(core, column), block(core, column), pot2_send, pot2_recv.at[d],
             {"band": (band // 4) * 4 + lax.rem(column + d, 4)},
+        )
+
+    hands_over = jnp.logical_and(is_chip, core == 1)
+
+    def across(d):
+        from_column = lax.rem(column + 4 - d, 4)
+        return remote(
+            block(1, from_column), block(1, from_column), pot3_send.at[d], pot3_recv, {"grid": level * 4 + 2 * row}
         )
 
     @pl.when(is_chip)
@@ -195,20 +203,17 @@
         for d in range(1, 4):
             along(d).start()
 
+        @pl.when(core == 1)
+        def _():
+            across(0).start()
+
     send_vectors(4, 12)
 
-    across = remote(
-        block(1, 0, 4), block(1, 0, 4), pot3_send, pot3_recv, {"grid": level * 4 + 2 * row}
-    )
-    hands_over = jnp.logical_and(is_chip, core == 1)
-
-    @pl.when(is_chip)
-    def _():
-        wait(block(0, 0, 3), pot2_recv)
-
-        @pl.when(hands_over)
-        def _():
-            across.start()
+    @pl.when(hands_over)
+    def _():
+        for d in (1, 3, 2):
+            wait(block(0, 0), pot2_recv.at[d])
+            across(d).start()
 
     for v, target in enumerate(ORB_OWNER + STO_OWNER):
         @pl.when(me != target)
@@ -270,15 +275,21 @@
         for d in range(1, 8):
             remote(own_mar, eight(ms, band), ms_send, ms_recv, {"band": lax.rem(band + d, BANDS)}).start()
 
-    services = (service_partial, service_slab, service_whole)
-
     @pl.when(jnp.logical_not(is_owner))
     def _():
-        for service in services:
-            service()
+        service_partial()
+        service_slab()
+
+    def forward_orbitals():
+        wait(orb_home, oh_recv)
+        own_cells(orb_home, a_f, 4, af_recv)
+        for d in range(1, 8):
+            cells(orb_home, a_f, 4, lax.rem(band + d, BANDS), af_send, af_recv).start()
 
     @pl.when(is_owner)
     def _():
+        for d in range(1, 4):
+            wait(block(0, 0), pot2_recv.at[d])
         wait(block(0, 0, 4), pot3_recv)
         small = lax.broadcasted_iota(jnp.int32, (16, 128), 1)
 
@@ -322,31 +333,36 @@
 
         @pl.loop(1, ORDER - 1)
         def _(k):
-            for at, service in enumerate(services[:2]):
-                @pl.when(jnp.logical_and(is_sto, k == 3 + at))
-                def _():
-                    service()
+            @pl.when(jnp.logical_and(is_sto, k == ORDER - 2))
+            def _():
+                service_partial()
 
             apply_operator(k, lax.rem(k, 2), 1 - lax.rem(k, 2), UY, None, *fields)
+
+        @pl.when(is_sto)
+        def _():
+            service_slab()
+
+        def give(to, home, at, recv):
+            slab = land.at[pl.ds(3 * to, 3)]
+
+            @pl.when(to != me)
+            def _():
+                remote(slab, home.at[:, :, at, :], out_send, recv, {"grid": to}).start()
+
+            @pl.when(to == me)
+            def _():
+                pltpu.make_async_copy(slab, home.at[:, :, at, :], recv).start()
 
         def hand_back(base):
             for u in range(12):
                 x = base + u
                 for k, part in enumerate(pack([FI[quarter(x, j), :] for j in range(4)], lane)):
                     land[x, pl.ds(k, 24, stride=3), :] = part
-            for u in range(4):
-                to = base // 3 + u
-                slab = land.at[pl.ds(3 * to, 3)]
-                for kind, home, at, recv in (
-                    (is_orb, orb_home, level // 2, oh_recv), (is_sto, sto_home, level, sh_recv)
-                ):
-                    @pl.when(jnp.logical_and(kind, to != me))
-                    def _():
-                        remote(slab, home.at[:, :, at, :], out_send, recv, {"grid": to}).start()
-
-                    @pl.when(jnp.logical_and(kind, to == me))
-                    def _():
-                        pltpu.make_async_copy(slab, home.at[:, :, at, :], recv).start()
+            @pl.when(is_orb)
+            def _():
+                for u in range(4):
+                    give(base // 3 + u, orb_home, level // 2, oh_recv)
 
         apply_operator(ORDER - 1, 1, 0, 6, hand_back, *fields)
 
@@ -355,12 +371,20 @@
             service_partial()
             service_slab()
 
+        @pl.when(is_sto)
+        def _():
+            service_whole()
+            forward_orbitals()
+
+            @pl.loop(0, 32)
+            def _(d):
+                give(lax.rem(me + d, 32), sto_home, level, sh_recv)
+
+    @pl.when(jnp.logical_not(is_sto))
+    def _():
         service_whole()
-
-    wait(orb_home, oh_recv)
-    own_cells(orb_home, a_f, 4, af_recv)
-    for d in range(1, 8):
-        cells(orb_home, a_f, 4, lax.rem(band + d, BANDS), af_send, af_recv).start()
+        forward_orbitals()
+
     wait(ms, ms_recv)
     m_high, m_low = halves(ms[:, 0:32] * (1.0 / SCALE))
     wait(a_f, af_recv)
@@ -421,7 +445,8 @@
 
         @pl.when(hands_over)
         def _():
-            across.wait_send()
+            for d in range(4):
+                across(d).wait_send()
 
     wait(orb.at[:, pl.ds(0, 7 * CHUNK)], ao_send)
     wait(sto.at[:, pl.ds(0, 7 * CHUNK)], as_send)
@@ -525,7 +550,7 @@
             pltpu.VMEM((3, ROWS, 8, 128), f32),
             pltpu.VMEM((BANDS, 3 * CHUNK, 128), f32),
             pltpu.VMEM((BANDS, 3 * CHUNK, 128), f32),
-            dma((12,)), dma((16,)), dma, dma, dma, dma, dma, dma, dma,
+            dma((12,)), dma((16,)), dma, dma, dma((4,)), dma((4,)), dma, dma, dma,
             dma, dma, dma, dma, dma, dma, dma, dma, dma, dma,
             dma, dma, dma, dma, dma, dma, dma, dma, dma,
         ],

time: 173 us -> 178 us (1.029)
  Pallas kernels: 164 us -> 168 us
    pallas_call x1, Pallas kernels: 164 us -> 168 us  [local(): pl.pallas_call(everything, out_shape=(jax.ShapeDtypeStruct((3, ROWS, 8, 1...]
where the time goes in v4:
time: 178 us; the launch traced here: 175 us
  Pallas kernels  168 us (94%)
  local copies, waits for them, and re-layouts  6.26 us (4%)
    pallas_call x1, Pallas kernels, local(): pl.pallas_call(everything, out_shape=(jax.ShapeDtypeStruct((3, ROWS, 8, 1...  168 us
    unnamed x6, local copies, waits for them, and re-layouts  5.02 us

profile of v4, /device:TPU:2, one launch (start us, length us, event | category | flops | bytes accessed | tf_op | source)
XLA Modules:
  0.0 175.1 jit_solution(17439518584277850070)
XLA Ops:
  0.6 0.0 copy-start
  0.7 0.9 copy-done
  1.6 0.6 pad.4.potc
  2.2 168.1 %shard_map.94 = (f32[3,72,8,128]{3,2,1,0:T(8,128)}, f32[8,128]{1,0:T(8,128)}, f32[3,1152]{1,0:T(4,128)}) custom-call(f32[3,72,4,128]{3,2,1,0:T(4,128)} %bitcast.13, s32[3,72,8,128]{3,2,1,0:T(8,128)} %bitcast.11, f32[56,128]{1,0:T(8,128)} %pad.4.potc, bf16[192,192]{1,0:T(8,128)(2,1)} %constant.30.clone.kx, bf16[192,192]{1,0:T(8,128)(2,1)} %constant.31.clone.ky, ...), custom_call_target="tpu_custom_call" | custom-call | tf_op jit(solution)/shard_map/pallas_call | solution.py:523
  170.3 0.0 copy-start.1
  170.3 0.7 copy-done.1
  171.0 0.6 slice_bitcast_fusion
  171.6 1.3 copy.12
  172.9 2.1 %copy.13 = f32[8,3,9216]{2,0,1:T(8,128)} copy(f32[8,3,9216]{2,0,1:T(8,128)} %bitcast.12) | data formatting | bytes 1769472
  (2 shorter events, 0.0 us)
Async XLA Ops:
  0.6 0.9 copy-start
  170.3 0.7 copy-start.1

commit v5 on v4

--- a/solution.py
+++ b/solution.py
@@ -280,12 +280,6 @@
         service_partial()
         service_slab()
 
-    def forward_orbitals():
-        wait(orb_home, oh_recv)
-        own_cells(orb_home, a_f, 4, af_recv)
-        for d in range(1, 8):
-            cells(orb_home, a_f, 4, lax.rem(band + d, BANDS), af_send, af_recv).start()
-
     @pl.when(is_owner)
     def _():
         for d in range(1, 4):
@@ -343,26 +337,24 @@
         def _():
             service_slab()
 
-        def give(to, home, at, recv):
-            slab = land.at[pl.ds(3 * to, 3)]
-
-            @pl.when(to != me)
-            def _():
-                remote(slab, home.at[:, :, at, :], out_send, recv, {"grid": to}).start()
-
-            @pl.when(to == me)
-            def _():
-                pltpu.make_async_copy(slab, home.at[:, :, at, :], recv).start()
-
         def hand_back(base):
             for u in range(12):
                 x = base + u
                 for k, part in enumerate(pack([FI[quarter(x, j), :] for j in range(4)], lane)):
                     land[x, pl.ds(k, 24, stride=3), :] = part
-            @pl.when(is_orb)
-            def _():
-                for u in range(4):
-                    give(base // 3 + u, orb_home, level // 2, oh_recv)
+            for u in range(4):
+                to = base // 3 + u
+                slab = land.at[pl.ds(3 * to, 3)]
+                for kind, home, at, recv in (
+                    (is_orb, orb_home, level // 2, oh_recv), (is_sto, sto_home, level, sh_recv)
+                ):
+                    @pl.when(jnp.logical_and(kind, to != me))
+                    def _():
+                        remote(slab, home.at[:, :, at, :], out_send, recv, {"grid": to}).start()
+
+                    @pl.when(jnp.logical_and(kind, to == me))
+                    def _():
+                        pltpu.make_async_copy(slab, home.at[:, :, at, :], recv).start()
 
         apply_operator(ORDER - 1, 1, 0, 6, hand_back, *fields)
 
@@ -371,20 +363,11 @@
             service_partial()
             service_slab()
 
-        @pl.when(is_sto)
-        def _():
-            service_whole()
-            forward_orbitals()
-
-            @pl.loop(0, 32)
-            def _(d):
-                give(lax.rem(me + d, 32), sto_home, level, sh_recv)
-
-    @pl.when(jnp.logical_not(is_sto))
-    def _():
-        service_whole()
-        forward_orbitals()
-
+    service_whole()
+    wait(orb_home, oh_recv)
+    own_cells(orb_home, a_f, 4, af_recv)
+    for d in range(1, 8):
+        cells(orb_home, a_f, 4, lax.rem(band + d, BANDS), af_send, af_recv).start()
     wait(ms, ms_recv)
     m_high, m_low = halves(ms[:, 0:32] * (1.0 / SCALE))
     wait(a_f, af_recv)

time: 178 us -> 173 us (0.972)
  Pallas kernels: 168 us -> 164 us
    pallas_call x1, Pallas kernels: 168 us -> 164 us  [local(): pl.pallas_call(everything, out_shape=(jax.ShapeDtypeStruct((3, ROWS, 8, 1...]
where the time goes in v5:
time: 173 us; the launch traced here: 171 us
  Pallas kernels  164 us (95%)
  local copies, waits for them, and re-layouts  6.26 us (4%)
    pallas_call x1, Pallas kernels, local(): pl.pallas_call(everything, out_shape=(jax.ShapeDtypeStruct((3, ROWS, 8, 1...  164 us
    unnamed x6, local copies, waits for them, and re-layouts  5.02 us

profile of v5, /device:TPU:2, one launch (start us, length us, event | category | flops | bytes accessed | tf_op | source)
XLA Modules:
  0.0 170.8 jit_solution(3984418679654243329)
XLA Ops:
  0.6 0.0 copy-start
  0.7 0.9 copy-done
  1.6 0.6 pad.4.potc
  2.2 163.8 %shard_map.94 = (f32[3,72,8,128]{3,2,1,0:T(8,128)}, f32[8,128]{1,0:T(8,128)}, f32[3,1152]{1,0:T(4,128)}) custom-call(f32[3,72,4,128]{3,2,1,0:T(4,128)} %bitcast.13, s32[3,72,8,128]{3,2,1,0:T(8,128)} %bitcast.11, f32[56,128]{1,0:T(8,128)} %pad.4.potc, bf16[192,192]{1,0:T(8,128)(2,1)} %constant.30.clone.kx, bf16[192,192]{1,0:T(8,128)(2,1)} %constant.31.clone.ky, ...), custom_call_target="tpu_custom_call" | custom-call | tf_op jit(solution)/shard_map/pallas_call | solution.py:506
  166.0 0.0 copy-start.1
  166.0 0.7 copy-done.1
  166.7 0.6 slice_bitcast_fusion
  167.3 1.3 copy.12
  168.6 2.1 %copy.13 = f32[8,3,9216]{2,0,1:T(8,128)} copy(f32[8,3,9216]{2,0,1:T(8,128)} %bitcast.12) | data formatting | bytes 1769472
  (2 shorter events, 0.0 us)
Async XLA Ops:
  0.6 0.9 copy-start
  166.0 0.7 copy-start.1
